TPU v7x, 256 devices: a whole 4x4x8 slice. The times are simulated.
256 devices in a mesh: seq: 64 (over z, x, y_lo), kv: 4 (over y_hi, core).
Axes of the slice: x: 4, y: 4 (y_hi: 2, y_lo: 2; y = y_hi * 2 + y_lo), z: 8, core: 2. Of those that a mesh axis runs over, the one named last changes fastest.
Arguments:
- queries: bfloat16 [32768, 1024], P('seq'), may hold values from -88 to 88
- keys: bfloat16 [512, 64, 1024], P('seq', 'kv'), may hold values from -4 to 4
- values: bfloat16 [512, 64, 1024], P('seq', 'kv'), may hold values from -6 to 6
- layout: int32 [512, 71], replicated, may hold values from -1 to 511, as said below
- grad_out: bfloat16 [32768, 1024], P('seq'), may hold values from -6 to 6
Outputs:
- attended: bfloat16 [32768, 1024], P('seq')
- grad_q: bfloat16 [32768, 1024], P('seq')
- grad_k: bfloat16 [512, 64, 1024], P('seq', 'kv')
- grad_v: bfloat16 [512, 64, 1024], P('seq', 'kv')
Inputs may be any that keep to these rules, and one draw needn't show every extreme that they name: `layout`: write query block b as 8 w + i with 0 <= i < 8. Row b lists the summary block of each window 0 .. w - 1 in order of windows, then the blocks 8 w .. 8 w + i in order, then -1 in the remaining entries. The summary block of window u is one of the blocks 8 u .. 8 u + 7 and is the same in every row.
All inputs are finite; a program needn't handle non-finite values.
Results may differ from a plain program's by a relative error of at most 0.038.
Values may be sent and summed in bfloat16 or wider, within the bound.
A program may use at most 128 MiB of HBM per device.

v0:
```python
import math

import jax
import jax.numpy as jnp
from jax import lax
from jax.sharding import PartitionSpec as P

HEADS = 8


def head_major(rows, heads):
    return rows.reshape(rows.shape[0], heads, rows.shape[1] // heads).transpose(1, 0, 2)


def key_table(local_part, gathered, member):
    local_rows = local_part.reshape(-1, local_part.shape[-1])
    remote_rows = gathered[:, member].reshape(-1, gathered.shape[-1])
    return head_major(jnp.concatenate([local_rows, remote_rows], axis=0), HEADS)


def shards(queries, keys, values, layout, grad_out):
    seq_count = lax.axis_size("seq")
    seq_index = lax.axis_index("seq")
    kv_index = lax.axis_index("kv")
    tok_rows, feat_width = queries.shape
    blocks, part_tok = (keys.shape[0], keys.shape[1])
    blk_len = part_tok * lax.axis_size("kv")
    head_dim = feat_width // HEADS
    score_scale = 1.0 / math.sqrt(head_dim)
    last_row = layout[layout.shape[0] - 1]
    pick_window = jnp.minimum(seq_index, seq_count - 2)
    summary_local = jnp.clip(last_row[pick_window] - seq_index * blocks, 0, blocks - 1)
    own_pair = jnp.stack(
        [
            lax.dynamic_index_in_dim(keys, summary_local, 0, keepdims=False),
            lax.dynamic_index_in_dim(values, summary_local, 0, keepdims=False),
        ]
    )[None]
    row_pos = jnp.arange(tok_rows, dtype=jnp.int32)
    row_block = row_pos // blk_len
    row_tok = row_pos % blk_len
    local_pos = jnp.arange(blocks * part_tok, dtype=jnp.int32)
    key_block = local_pos // part_tok
    key_tok = kv_index * part_tok + local_pos % part_tok
    local_ok = (key_block[None, :] < row_block[:, None]) | (
        key_block[None, :] == row_block[:, None]
    ) & (key_tok[None, :] <= row_tok[:, None])
    remote_window = jnp.arange(seq_count * part_tok, dtype=jnp.int32) // part_tok
    remote_ok = jnp.broadcast_to(
        (remote_window < seq_index)[None, :], (tok_rows, remote_window.shape[0])
    )
    allowed = jnp.concatenate([local_ok, remote_ok], axis=1)
    gathered = lax.all_gather(own_pair, "seq", axis=0, tiled=True)
    key_heads = key_table(keys, gathered, 0)
    value_heads = key_table(values, gathered, 1)
    query_heads = head_major(queries, HEADS)
    grad_heads = head_major(grad_out, HEADS)

    def scores(query_rows, key_rows):
        return (
            jnp.einsum("rd,kd->rk", query_rows, key_rows, preferred_element_type=jnp.float32)
            * score_scale
        )

    def head_peak(head_items):
        return jnp.max(jnp.where(allowed, scores(head_items[0], head_items[1]), -jnp.inf), axis=1)

    row_max = lax.pmax(lax.map(head_peak, (query_heads, key_heads)), "kv")

    def head_mass(head_items):
        query_rows, key_rows, value_rows, row_peak = head_items
        weight = jnp.where(allowed, jnp.exp(scores(query_rows, key_rows) - row_peak[:, None]), 0.0)
        weighted = jnp.dot(
            weight.astype(jnp.bfloat16), value_rows, preferred_element_type=jnp.float32
        )
        return (jnp.sum(weight, axis=1), weighted)

    part_total, part_out = lax.map(head_mass, (query_heads, key_heads, value_heads, row_max))
    total_rows = part_total.T
    out_rows = part_out.transpose(1, 0, 2).reshape(tok_rows, feat_width)
    row_total, summed = lax.psum((total_rows, out_rows), "kv")
    attended = (
        (summed.reshape(tok_rows, HEADS, head_dim) / row_total[:, :, None])
        .reshape(tok_rows, feat_width)
        .astype(jnp.bfloat16)
    )
    row_delta = jnp.sum(
        (grad_out.astype(jnp.float32) * attended.astype(jnp.float32)).reshape(
            tok_rows, HEADS, head_dim
        ),
        axis=2,
    )
    regathered = lax.all_gather(own_pair, "seq", axis=0, tiled=True)
    key_heads = key_table(keys, regathered, 0)
    value_heads = key_table(values, regathered, 1)

    def head_grads(head_items):
        query_rows, key_rows, value_rows, grad_rows, row_peak, row_mass, row_drift = head_items
        probability = jnp.where(
            allowed,
            jnp.exp(scores(query_rows, key_rows) - row_peak[:, None]) / row_mass[:, None],
            0.0,
        )
        grad_prob = jnp.einsum(
            "rd,kd->rk", grad_rows, value_rows, preferred_element_type=jnp.float32
        )
        grad_score = (score_scale * probability * (grad_prob - row_drift[:, None])).astype(
            jnp.bfloat16
        )
        query_grad = jnp.dot(grad_score, key_rows, preferred_element_type=jnp.float32)
        key_grad = jnp.einsum(
            "rk,rd->kd", grad_score, query_rows, preferred_element_type=jnp.float32
        )
        value_grad = jnp.einsum(
            "rk,rd->kd",
            probability.astype(jnp.bfloat16),
            grad_rows,
            preferred_element_type=jnp.float32,
        )
        return (query_grad, key_grad, value_grad)

    query_grad, key_grad, value_grad = lax.map(
        head_grads,
        (query_heads, key_heads, value_heads, grad_heads, row_max, row_total.T, row_delta.T),
    )
    grad_q = lax.psum(query_grad.transpose(1, 0, 2).reshape(tok_rows, feat_width), "kv").astype(
        jnp.bfloat16
    )
    key_count = key_grad.shape[1]
    key_rows_grad = key_grad.transpose(1, 0, 2).reshape(key_count, feat_width)
    value_rows_grad = value_grad.transpose(1, 0, 2).reshape(key_count, feat_width)
    local_count = blocks * part_tok
    window_term = jnp.stack(
        [
            key_rows_grad[local_count:].reshape(seq_count, part_tok, feat_width),
            value_rows_grad[local_count:].reshape(seq_count, part_tok, feat_width),
        ],
        axis=1,
    )
    arrived = lax.psum_scatter(window_term, "seq", scatter_dimension=0, tiled=True)
    chosen = (jnp.arange(blocks) == summary_local)[:, None, None]
    grad_k = (
        key_rows_grad[:local_count].reshape(blocks, part_tok, feat_width)
        + jnp.where(chosen, arrived[0, 0][None], 0.0)
    ).astype(jnp.bfloat16)
    grad_v = (
        value_rows_grad[:local_count].reshape(blocks, part_tok, feat_width)
        + jnp.where(chosen, arrived[0, 1][None], 0.0)
    ).astype(jnp.bfloat16)
    return (attended, grad_q, grad_k, grad_v)


def solution(mesh):
    return jax.shard_map(
        shards,
        mesh=mesh,
        in_specs=(P("seq", None), P("seq", "kv", None), P("seq", "kv", None), P(), P("seq", None)),
        out_specs=(P("seq", None), P("seq", None), P("seq", "kv", None), P("seq", "kv", None)),
        check_vma=False,
    )
```

profile of v0, /device:TPU:16, one launch (start us, length us, event | category | flops | bytes accessed | tf_op | source)
XLA Modules:
  0.0 1226.9 jit_solution(6416667151091115999)
XLA Ops:
  15.1 302.7 %all-gather.3.cloned.1.call-done = bf16[128,16,1024]{2,1,0:T(8,128)(2,1)} async-done(((bf16[2,16,1024]{2,1,0:T(8,128)(2,1)}), bf16[128,16,1024]{2,1,0:T(8,128)(2,1)}) %all-gather.3.cloned.1.call-update) | async-done | bytes 4194320 | tf_op jit(solution)/shard_map/all_gather | solution.py:53
  317.8 2.7 fusion.70
  321.5 1.9 maximum_bitcast_fusion
  323.3 1.8 copy.40
  325.1 15.1 %while.36 = (s32[]{:T(128)}, f32[8,512]{1,0:T(8,128)S(1)}, bf16[8,512,128]{2,1,0:T(8,128)(2,1)S(1)}, bf16[8,1152,128]{2,1,0:T(8,128)(2,1)}, pred[512,1152]{1,0:T(32,128)(4,1)}, /*index=5*/s32[]{:T(128)}, s32[]{:T(128)}) while((s32[]{:T(128)}, f32[8,512]{1,0:T(8,128)S(1)}, bf16[8,512,128]{2,1,0:T(8,128)(2,1)S(1)}, ...), condition=%wide.region_2.3_spmd, body=%wide.region_0.2_spmd.sunk | while | flops 152763904 | bytes 1023065 | solution.py:68
  325.1 1.8 fusion.100
  327.0 1.8 fusion.100
  328.9 1.8 fusion.100
  330.8 1.8 fusion.100
  332.7 1.8 fusion.100
  334.6 1.8 fusion.100
  336.5 1.8 fusion.100
  338.4 1.8 fusion.100
  340.3 13.1 %pmax.7 = f32[8,512]{1,0:T(8,128)S(1)} all-reduce(f32[8,512]{1,0:T(8,128)S(1)} %get-tuple-element.138), channel_id=1, replica_groups=mesh['seq'=64,'kv'=4] {'kv'}, use_global_device_ids=true, to_apply=%region_3.4 | all-reduce | flops 4096 | bytes 32768 | tf_op jit(solution)/shard_map/pmax | solution.py:68
  354.1 1.9 maximum_bitcast_fusion.1
  358.4 42.0 %while.37 = (s32[]{:T(128)}, f32[8,512]{1,0:T(8,128)}, f32[8,512,128]{2,1,0:T(8,128)}, bf16[8,512,128]{2,1,0:T(8,128)(2,1)}, bf16[8,1152,128]{2,1,0:T(8,128)(2,1...) while((s32[]{:T(128)}, f32[8,512]{1,0:T(8,128)}, ...), condition=%wide.region_6.7_spmd, body=%wide.region_4.6_spmd.sunk | while | flops 304938496 | bytes 3946613 | solution.py:78
  358.4 2.7 fusion.103
  363.7 2.7 fusion.103
  369.0 2.7 fusion.103
  374.2 2.7 fusion.103
  379.5 2.7 fusion.103
  384.7 2.7 fusion.103
  390.0 2.7 fusion.103
  395.2 2.7 fusion.103
  400.5 3.2 copy_bitcast_fusion.1
  405.2 13.9 %psum.22 = f32[512,8]{0,1:T(8,128)S(1)} all-reduce(f32[512,8]{0,1:T(8,128)S(1)} %bitcast.197), channel_id=1, replica_groups=mesh['seq'=64,'kv'=4] {'kv'}, use_global_device_ids=true, to_apply=%region_8.9 | all-reduce | flops 4096 | bytes 32768 | tf_op jit(solution)/shard_map/psum | solution.py:81
  420.0 42.3 %all-reduce.5.cloned.1.call-done = f32[512,1024]{1,0:T(8,128)} async-done(((f32[512,1024]{1,0:T(8,128)}), f32[512,1024]{1,0:T(8,128)}) %all-reduce.5.cloned.1.call-update) | async-done | bytes 2097168 | tf_op jit(solution)/shard_map/psum | solution.py:81
  463.9 3.4 multiply_bitcast_fusion
  467.4 1.8 copy.67
  469.1 2.9 reduce_sum.18
  474.6 67.7 %while.38 = (s32[]{:T(128)}, f32[8,512,128]{2,1,0:T(8,128)}, f32[8,1152,128]{2,1,0:T(8,128)}, f32[8,1152,128]{2,1,0:T(8,128)}, bf16[8,512,128]{2,1,0:T(8,128)(2,...) while((s32[]{:T(128)}, f32[8,512,128]{2,1,0:T(8,128)}, ...), condition=%wide.region_11.12_spmd, body=%wide.region_10.11_spmd.sunk | while | flops 760283136 | bytes 14081165 | solution.py:122
  474.6 2.1 fusion.115
  477.3 2.1 fusion.117
  479.5 2.3 fusion.118
  483.1 2.0 fusion.115
  485.8 2.1 fusion.117
  487.9 2.3 fusion.118
  491.6 2.0 fusion.115
  494.2 2.1 fusion.117
  496.4 2.3 fusion.118
  500.1 2.1 fusion.115
  502.7 2.1 fusion.117
  504.9 2.2 fusion.118
  508.5 2.0 fusion.115
  511.2 2.2 fusion.117
  513.3 2.2 fusion.118
  516.9 2.0 fusion.115
  519.6 2.2 fusion.117
  521.8 2.2 fusion.118
  525.4 2.0 fusion.115
  528.1 2.2 fusion.117
  530.2 2.2 fusion.118
  533.9 2.0 fusion.115
  536.6 2.1 fusion.117
  538.7 2.2 fusion.118
  542.3 2.5 slice.46
  544.8 4.4 copy.53
  549.2 4.9 stack_reshape.7
  554.1 2.5 slice.45
  556.6 4.4 copy.52
  561.0 4.9 stack_reshape.6
  565.9 8.4 pad_maximum_fusion
  583.8 92.1 %all-reduce.8 = bf16[512,1024]{1,0:T(8,128)(2,1)} all-reduce(f32[512,1024]{1,0:T(8,128)S(1)} %copy-done.1), channel_id=1, replica_groups=mesh['seq'=64,'kv'=4] {'kv'}, use_global_device_ids=true, to_apply=%region_12.13 | all-reduce | flops 524288 | bytes 3145728 | tf_op jit(solution)/shard_map/psum | solution.py:126
  675.8 542.0 %all-reduce.7.cloned.1.call-done = f32[64,2,16,1024]{3,2,0,1:T(8,128)} async-done(((f32[64,2,16,1024]{3,2,0,1:T(8,128)}), f32[64,2,16,1024]{3,2,0,1:T(8,128)}) %all-reduce.7.cloned.1.call-update) | async-done | bytes 8388624
  (126 shorter events, 66.5 us)
Async XLA Ops:
  7.2 5.8 copy-start.5
  7.2 310.6 %all-gather.3.cloned.1.call-start = ((), (), s32[]{:S(2)}) async-start(), calls=%async_computation.1 | async-start | bytes 4259840 | tf_op jit(solution)/shard_map/all_gather | solution.py:53
  10.7 451.6 %all-reduce.5.cloned.1.call-start = ((), (), s32[]{:S(2)}) async-start(), calls=%async_computation | async-start | bytes 4194304 | tf_op jit(solution)/shard_map/psum | solution.py:81
  10.8 3.0 copy-start.6
  320.5 1.0 copy-start.4
  340.3 13.8 %copy-start.3 = (bf16[8,512,128]{2,1,0:T(8,128)(2,1)}, bf16[8,512,128]{2,1,0:T(8,128)(2,1)S(1)}, u32[]{:S(2)}) copy-start(bf16[8,512,128]{2,1,0:T(8,128)(2,1)S(1)} %get-tuple-element.526) | copy-start | bytes 3145732
  403.6 1.6 copy-start.7
  403.7 814.2 %all-reduce.7.cloned.1.call-start = ((), (), s32[]{:S(2)}) async-start(), calls=%async_computation.2 | async-start | bytes 16777216
  462.3 1.6 copy-start.2
  574.2 0.7 copy-start.8
  574.3 3.4 copy-start
  579.3 4.5 copy-start.1
Sparse Core Ops, SparseCore 0:
  10.8 306.9 all-gather.2
  403.8 58.4 all-reduce.4
  574.4 643.4 all-reduce.6
where the time goes:
time: 1230 us
  waiting for transfers between devices  887 us (72%)
  blocking collectives  119 us (10%)
  matrix products  113 us (9%)
  local copies, waits for them, and re-layouts  71 us (6%)
  other arithmetic  21.4 us (2%)
  between operations  14.7 us (1%)
    unnamed x4, waiting for transfers between devices  542 us
    all_gather x1, waiting for transfers between devices, shards(): gathered = lax.all_gather(own_pair, 'seq', axis=0, tiled=True)  303 us
    psum x1, blocking collectives, shards(): lax.psum(query_grad.transpose(1, 0, 2).reshape(tok_rows, feat_width), 'kv')  92.1 us
    dot_general x24, matrix products, scores(): jnp.einsum('rd,kd->rk', query_rows, key_rows, preferred_element_type=jnp....  52.6 us
    psum x1, waiting for transfers between devices, shards(): row_total, summed = lax.psum((total_rows, out_rows), 'kv')  42.3 us
  transfers between devices with their start and end apart: 3, of which 3 were waited for; matrix products, arithmetic and copies ran while one was open for 1% of the time, Pallas kernels for 0%

commit v1 on v0

v1 whole, which is shorter than its diff:
```python
import functools
import math

import jax
import jax.numpy as jnp
from jax import lax
from jax.experimental import pallas as pl
from jax.experimental.pallas import tpu as pltpu
from jax.sharding import PartitionSpec as P

HD = 128
PLANE = 8
MESH = pl.DeviceIdType.MESH
F32 = jnp.float32
BF16 = jnp.bfloat16
SCALE = 1.0 / math.sqrt(HD)
LOG2_SCALE = math.log2(math.e) / math.sqrt(HD)
NT = (((1,), (1,)), ((), ()))
NN = (((1,), (0,)), ((), ()))
TN = (((0,), (0,)), ((), ()))
KEY_TILE = 256


def dot(a, b, dims):
    return lax.dot_general(a, b, dims, preferred_element_type=F32)


def kernel(
    nz, layout_ref, q_hbm, k_in, v_in, do_hbm,
    att_out, dq_out, dk_out, dv_out,
    q, do, sums, ag, grad, m, l, acc, lse_row, delta_row, dqt, att, dq, fin,
    sk1, sk2, sk3, sv1, sv2, sv3, sz, rk1, rk2, rk3, rv1, rv2, rv3, rz, own,
    load_sem, sum_s, sum_r, kv_s, kv_r, zs, zr, ag_s, ag_r, rs_s, rs_r, gz_s, gz_r,
    att_s, att_r, dq_s, dq_r, fin_s, fin_r, loc_sem,
):
    tok, width = q.shape
    heads = width // HD
    blocks, part_tok = k_in.shape[0], k_in.shape[1]
    blk = ag.shape[3]
    half = blk // 2
    n_kv = lax.axis_size("kv")
    s = lax.axis_index("seq")
    k = lax.axis_index("kv")
    z, r = s // PLANE, s % PLANE
    x, y = r // 2, r % 2
    left, right, opp, yo = (x + 3) % 4, (x + 1) % 4, (x + 2) % 4, 1 - y
    base = z * PLANE
    dev_left = {"seq": base + left * 2 + y}
    dev_right = {"seq": base + right * 2 + y}
    dev_y = {"seq": base + x * 2 + yo}
    peers = [(k + i) % n_kv for i in range(1, n_kv)]
    cols = pl.ds(pl.multiple_of(k * width, width), width)

    def peer_cols(p):
        return pl.ds(pl.multiple_of(p * width, width), width)

    def part(p):
        return pl.ds(pl.multiple_of(p * part_tok, part_tok), part_tok)

    def rcopy(src, dst, send, recv, dev):
        return pltpu.make_async_remote_copy(
            src_ref=src, dst_ref=dst, send_sem=send, recv_sem=recv, device_id=dev, device_id_type=MESH
        )

    load_q = pltpu.make_async_copy(q_hbm.at[:, cols], q, load_sem.at[0])
    load_do = pltpu.make_async_copy(do_hbm.at[:, cols], do, load_sem.at[1])
    load_q.start()
    load_do.start()
    barrier = pltpu.get_barrier_semaphore()
    for p in peers:
        pl.semaphore_signal(barrier, inc=1, device_id={"kv": p}, device_id_type=MESH)
    for dev in (dev_left, dev_right, dev_y):
        pl.semaphore_signal(barrier, inc=1, device_id=dev, device_id_type=MESH)
    for i in range(1, nz):
        pl.semaphore_signal(
            barrier, inc=1, device_id={"seq": ((z + i) % nz) * PLANE + r}, device_id_type=MESH
        )
    summary = jnp.clip(
        layout_ref[layout_ref.shape[0] - 1, jnp.minimum(s, nz * PLANE - 2)] - s * blocks, 0, blocks - 1
    )
    sums[0] = k_in[summary]
    sums[1] = v_in[summary]
    pl.semaphore_wait(barrier, len(peers) + 3 + nz - 1)

    def sum_copy(p, slot):
        return rcopy(
            sums.at[:, :, peer_cols(p)], ag.at[z, :, r, part(slot)], sum_s.at[p], sum_r.at[slot], {"kv": p}
        )

    for p in peers:
        sum_copy(p, k).start()
    own_sum = pltpu.make_async_copy(sums.at[:, :, cols], ag.at[z, :, r, part(k)], loc_sem.at[0])
    own_sum.start()

    def kv_copy(t, p, slot):
        ref = (k_in, v_in)[t]
        return rcopy(
            ref.at[:, :, peer_cols(p)], ag.at[nz, t, :, part(slot)], kv_s.at[t, p], kv_r.at[t, slot], {"kv": p}
        )

    own_kv = [
        pltpu.make_async_copy(ref.at[:, :, cols], ag.at[nz, t, :, part(k)], loc_sem.at[1 + t])
        for t, ref in enumerate((k_in, v_in))
    ]
    for c in own_kv:
        c.start()
    own_sum.wait()
    for p in peers:
        sum_copy(p, p).wait_recv()

    def z_copy(dz):
        return rcopy(ag.at[z, :, r], ag.at[z, :, r], zs.at[dz], zr.at[z], {"seq": s + dz * PLANE})

    for dz in range(1, nz):
        @pl.when(z + dz < nz)
        def _(dz=dz):
            z_copy(dz).start()

    for t in range(2):
        for p in peers:
            kv_copy(t, p, k).start()

    def blk_x(o, t, xx, yy):
        return ag.at[o, t, xx * 2 + yy]

    def pair(o, xx):
        return ag.at[o, 0, pl.ds(xx * 2, 2)]

    def agc(o, i, ref, dev, j=None):
        j = i if j is None else j
        return rcopy(ref, ref, ag_s.at[o, i], ag_r.at[o, j], dev)

    def lo(ref):
        return ref.at[pl.ds(0, half)]

    def hi(ref):
        return ref.at[pl.ds(half, half)]

    def ag1(o):
        return [
            agc(o, 0, blk_x(o, 0, x, y), dev_y),
            agc(o, 1, blk_x(o, 1, x, y), dev_right),
            agc(o, 2, blk_x(o, 1, x, y), dev_left),
            agc(o, 3, blk_x(o, 1, x, y), dev_y, 10 + x),
        ]

    def ag1_in(o):
        return [
            agc(o, 0, blk_x(o, 0, x, yo), dev_y),
            agc(o, 1, blk_x(o, 1, left, y), dev_left),
            agc(o, 2, blk_x(o, 1, right, y), dev_right),
        ]

    def ag2(o):
        return [
            agc(o, 4, pair(o, x), dev_right),
            agc(o, 5, pair(o, x), dev_left),
            agc(o, 6, lo(blk_x(o, 1, left, y)), dev_right),
            agc(o, 7, hi(blk_x(o, 1, right, y)), dev_left),
            agc(o, 8, blk_x(o, 1, left, y), dev_y, 10 + left),
            agc(o, 9, blk_x(o, 1, right, y), dev_y, 10 + right),
        ]

    def ag2_in(o):
        return [
            agc(o, 4, pair(o, left), dev_left),
            agc(o, 5, pair(o, right), dev_right),
            agc(o, 6, lo(blk_x(o, 1, opp, y)), dev_left),
            agc(o, 7, hi(blk_x(o, 1, opp, y)), dev_right),
        ]

    def ag3(o):
        return [
            agc(o, 10, blk_x(o, 0, left, 0), dev_right, 8),
            agc(o, 11, blk_x(o, 0, right, 1), dev_left, 9),
            agc(o, 12, blk_x(o, 1, opp, y), dev_y, 10 + opp),
        ]

    def ag3_in(o):
        return [
            agc(o, 8, blk_x(o, 0, opp, 0), dev_left),
            agc(o, 9, blk_x(o, 0, opp, 1), dev_right),
        ] + [agc(o, 0, blk_x(o, 1, xx, yo), dev_y, 10 + xx) for xx in range(4)]

    def start(copies):
        for c in copies:
            c.start()

    def recv(copies):
        for c in copies:
            c.wait_recv()

    def sent(copies):
        for c in copies:
            c.wait_send()

    m[...] = jnp.full_like(m, -1e30)
    l[...] = jnp.zeros_like(l)
    acc[...] = jnp.zeros_like(acc)
    load_q.wait()
    load_do.wait()

    plane_keys = PLANE * blk

    def forward(c, slope, offset, masked):
        if masked:
            row = lax.broadcasted_iota(jnp.int32, (tok, 1), 0) * slope + offset
            lane = lax.broadcasted_iota(jnp.int32, (tok, HD), 1)
        for h in range(heads):
            hs = slice(h * HD, h * HD + HD)
            kk = ag[c, 0, :, :, hs].reshape(plane_keys, HD)
            vv = ag[c, 1, :, :, hs].reshape(plane_keys, HD)
            score = dot(q[:, hs], kk, NT) * LOG2_SCALE
            tiles = [score[:, j * HD : j * HD + HD] for j in range(plane_keys // HD)]
            if masked:
                tiles = [jnp.where(lane + j * HD <= row, t, -jnp.inf) for j, t in enumerate(tiles)]
            top = functools.reduce(jnp.maximum, tiles)
            m_old = m[h]
            m_new = jnp.maximum(m_old, jnp.max(top, axis=1, keepdims=True))
            alpha = jnp.exp2(m_old - m_new)
            weights = [jnp.exp2(t - m_new) for t in tiles]
            l[h] = l[h] * alpha + functools.reduce(jnp.add, weights)
            w = jnp.concatenate([t.astype(BF16) for t in weights], axis=1)
            acc[h] = acc[h] * alpha + dot(w, vv, NN)
            m[h] = m_new

    def fwd_step(it, _):
        @pl.when(it <= z)
        def _():
            o = z - it

            @pl.when(it > 0)
            def _():
                rcopy(ag.at[o, :, r], ag.at[o, :, r], zs.at[0], zr.at[o], dev_y).wait_recv()

            start(ag1(o))

        @pl.when((it >= 1) & (it - 1 <= z))
        def _():
            o = z - (it - 1)
            recv(ag1_in(o))
            start(ag2(o))

        @pl.when((it >= 2) & (it - 2 <= z))
        def _():
            o = z - (it - 2)
            recv(ag2_in(o))
            start(ag3(o))

        @pl.when(it == 0)
        def _():
            for c in own_kv:
                c.wait()
            for t in range(2):
                for p in peers:
                    kv_copy(t, p, p).wait_recv()

        @pl.when(it >= 3)
        def _():
            recv(ag3_in(z - (it - 3)))

        @pl.when((it == 0) | (it == 3))
        def _():
            local = it == 0
            forward(
                jnp.where(local, nz, z), jnp.where(local, 1, 0), jnp.where(local, 0, r * blk - 1), True
            )

        @pl.when(it > 3)
        def _():
            forward(z - (it - 3), 0, 0, False)

        return 0

    lax.fori_loop(0, z + 4, fwd_step, 0)

    for h in range(heads):
        hs = slice(h * HD, h * HD + HD)
        total = jnp.sum(l[h], axis=1, keepdims=True)
        out = (acc[h] / total).astype(BF16)
        att[:, hs] = out
        delta = jnp.sum(out.astype(F32) * do[:, hs].astype(F32), axis=1, keepdims=True)
        lse_row[h] = jnp.transpose(m[h] + jnp.log2(total))[:8]
        delta_row[h] = jnp.transpose(jnp.broadcast_to(delta, (tok, HD)))[:8]

    def out_copy(src, dst, send, recv_, p, slot):
        return rcopy(src, dst.at[:, peer_cols(slot)], send.at[p], recv_.at[slot], {"kv": p})

    for p in peers:
        out_copy(att, att_out, att_s, att_r, p, k).start()
    own_att = pltpu.make_async_copy(att, att_out.at[:, cols], loc_sem.at[3])
    own_att.start()

    dqt[...] = jnp.zeros_like(dqt)

    def backward(c, slope, offset, masked):
        tile_blocks = KEY_TILE // blk
        for h in range(heads):
            hs = slice(h * HD, h * HD + HD)
            lse = lse_row[h, 0:1, :]
            delta = delta_row[h, 0:1, :]
            qh, doh = q[:, hs], do[:, hs]
            for t in range(plane_keys // KEY_TILE):
                bs = slice(t * tile_blocks, (t + 1) * tile_blocks)
                kk = ag[c, 0, bs, :, hs].reshape(KEY_TILE, HD)
                vv = ag[c, 1, bs, :, hs].reshape(KEY_TILE, HD)
                prob = jnp.exp2(dot(kk, qh, NT) * LOG2_SCALE - lse)
                if masked:
                    row = lax.broadcasted_iota(jnp.int32, (1, tok), 1) * slope + offset
                    key = lax.broadcasted_iota(jnp.int32, (KEY_TILE, tok), 0) + t * KEY_TILE
                    prob = jnp.where(key <= row, prob, 0.0)
                ds = (prob * (dot(vv, doh, NT) - delta)).astype(BF16)
                grad[c, 1, bs, :, hs] = dot(prob.astype(BF16), doh, NN).reshape(tile_blocks, blk, HD)
                grad[c, 0, bs, :, hs] = (dot(ds, qh, NN) * SCALE).reshape(tile_blocks, blk, HD)
                dqt[h] += dot(kk, ds, TN)

    def rsc(o, i, src, dst, dev):
        return rcopy(src, dst, rs_s.at[o, i], rs_r.at[o, i], dev)

    def rs1(o):
        return [
            rsc(o, 0, sk1.at[o, 0], rk1.at[o, 0], dev_left),
            rsc(o, 1, sk1.at[o, 1], rk1.at[o, 1], dev_right),
            rsc(o, 2, sv1.at[o], rv1.at[o], dev_y),
        ]

    def rs2(o):
        return [
            rsc(o, 3, sk2.at[o, 0], rk2.at[o, 0], dev_left),
            rsc(o, 4, sk2.at[o, 1], rk2.at[o, 1], dev_right),
            rsc(o, 5, sv2.at[o, 0], rv2.at[o, 0], dev_left),
            rsc(o, 6, sv2.at[o, 1], rv2.at[o, 1], dev_right),
        ]

    def rs3(o):
        return [
            rsc(o, 7, sk3.at[o], rk3.at[o], dev_y),
            rsc(o, 8, sv3.at[o, 0], rv3.at[o, 0], dev_left),
            rsc(o, 9, sv3.at[o, 1], rv3.at[o, 1], dev_right),
        ]

    def gz_copy(o):
        return rcopy(sz.at[o], rz.at[z], gz_s.at[o], gz_r.at[z], {"seq": o * PLANE + r})

    def reduce1(o):
        sk1[o, 0] = grad[o, 0, opp * 2].astype(BF16)
        sk1[o, 1] = grad[o, 0, opp * 2 + 1].astype(BF16)
        for xx in range(4):
            sv1[o, xx] = grad[o, 1, xx * 2 + yo].astype(BF16)
        start(rs1(o))

    def reduce2(o):
        recv(rs1(o))
        sk2[o, 0, 0] = (grad[o, 0, left * 2] + rk1[o, 0].astype(F32)).astype(BF16)
        sk2[o, 0, 1] = grad[o, 0, left * 2 + 1].astype(BF16)
        sk2[o, 1, 0] = grad[o, 0, right * 2].astype(BF16)
        sk2[o, 1, 1] = (grad[o, 0, right * 2 + 1] + rk1[o, 1].astype(F32)).astype(BF16)
        for xx in range(4):
            grad[o, 1, xx * 2 + y] += rv1[o, xx].astype(F32)
        far = grad[o, 1, opp * 2 + y].astype(BF16)
        sv2[o, 0] = far[:half]
        sv2[o, 1] = far[half:]
        start(rs2(o))

    def reduce3(o):
        recv(rs2(o))
        for yy in range(2):
            grad[o, 0, x * 2 + yy] += rk2[o, 0, yy].astype(F32) + rk2[o, 1, yy].astype(F32)
        sk3[o] = grad[o, 0, x * 2 + yo].astype(BF16)
        sv3[o, 0, :half] = (grad[o, 1, left * 2 + y, :half] + rv2[o, 0].astype(F32)).astype(BF16)
        sv3[o, 0, half:] = grad[o, 1, left * 2 + y, half:].astype(BF16)
        sv3[o, 1, :half] = grad[o, 1, right * 2 + y, :half].astype(BF16)
        sv3[o, 1, half:] = (grad[o, 1, right * 2 + y, half:] + rv2[o, 1].astype(F32)).astype(BF16)
        start(rs3(o))

    def reduce4(o):
        recv(rs3(o))
        own[0] = grad[o, 0, r] + rk3[o].astype(F32)
        own[1] = grad[o, 1, r] + (rv3[o, 0].astype(F32) + rv3[o, 1].astype(F32))

        @pl.when(o < z)
        def _():
            sz[o] = own[...].astype(BF16)
            gz_copy(o).start()

    def bwd_step(it, _):
        @pl.when(it < z)
        def _():
            backward(it, 0, 0, False)

        @pl.when((it == z) | (it == z + 1))
        def _():
            local = it > z
            backward(
                jnp.where(local, nz, z), jnp.where(local, 1, 0), jnp.where(local, 0, r * blk - 1), True
            )

        @pl.when(it <= z)
        def _():
            reduce1(it)

        @pl.when(it == z + 1)
        def _():
            for h in range(heads):
                hs = slice(h * HD, h * HD + HD)
                dq[:, hs] = jnp.transpose(dqt[h] * SCALE).astype(BF16)
            for p in peers:
                out_copy(dq, dq_out, dq_s, dq_r, p, k).start()
            pltpu.make_async_copy(dq, dq_out.at[:, cols], loc_sem.at[4]).start()

        @pl.when(it >= 3)
        def _():
            reduce4(it - 3)

        @pl.when((it >= 2) & (it - 2 <= z))
        def _():
            reduce3(it - 2)

        @pl.when((it >= 1) & (it - 1 <= z))
        def _():
            reduce2(it - 1)

        return 0

    lax.fori_loop(0, z + 4, bwd_step, 0)

    def add_plane(o, _):
        rcopy(sz.at[0], rz.at[o], gz_s.at[0], gz_r.at[o], dev_y).wait_recv()
        own[...] += rz[o].astype(F32)
        return 0

    lax.fori_loop(z + 1, nz, add_plane, 0)
    for t in range(2):
        for b in range(blocks):
            chosen = jnp.where(summary == b, own[t], 0.0)
            fin[t, b] = (grad[nz, t, b] + chosen).astype(BF16)

    def fin_copy(t, p, slot):
        out = (dk_out, dv_out)[t]
        return rcopy(
            fin.at[t, :, part(p)], out.at[:, :, peer_cols(slot)], fin_s.at[t, p], fin_r.at[t, slot], {"kv": p}
        )

    own_fin = [
        pltpu.make_async_copy(fin.at[t, :, part(k)], ref.at[:, :, cols], loc_sem.at[5 + t])
        for t, ref in enumerate((dk_out, dv_out))
    ]
    for t in range(2):
        for p in peers:
            fin_copy(t, p, k).start()
        own_fin[t].start()

    for p in peers:
        sum_copy(p, k).wait_send()
        for t in range(2):
            kv_copy(t, p, k).wait_send()
    for dz in range(1, nz):
        @pl.when(z + dz < nz)
        def _(dz=dz):
            z_copy(dz).wait_send()

    def sent_step(o, _):
        sent(ag1(o) + ag2(o) + ag3(o) + rs1(o) + rs2(o) + rs3(o))

        @pl.when(o < z)
        def _():
            gz_copy(o).wait_send()

        return 0

    lax.fori_loop(0, z + 1, sent_step, 0)
    own_att.wait()
    pltpu.make_async_copy(dq, dq_out.at[:, cols], loc_sem.at[4]).wait()
    for p in peers:
        for src, dst, send, recv_ in ((att, att_out, att_s, att_r), (dq, dq_out, dq_s, dq_r)):
            out_copy(src, dst, send, recv_, p, k).wait_send()
            out_copy(src, dst, send, recv_, p, p).wait_recv()
    for t in range(2):
        own_fin[t].wait()
        for p in peers:
            fin_copy(t, p, k).wait_send()
            fin_copy(t, p, p).wait_recv()


def shards(queries, keys, values, layout, grad_out):
    tok, feat = queries.shape
    blocks, part_tok = keys.shape[0], keys.shape[1]
    n_kv = lax.axis_size("kv")
    nz = lax.axis_size("seq") // PLANE
    blk = part_tok * n_kv
    width = feat // n_kv
    heads = width // HD
    rows, entries = layout.shape
    any_spec = pl.BlockSpec(memory_space=pl.ANY)
    whole = pl.BlockSpec(keys.shape, lambda i: (0, 0, 0))
    dma = pltpu.SemaphoreType.DMA

    def vm(*shape, dtype=BF16):
        return pltpu.VMEM(shape, dtype)

    half = blk // 2
    return pl.pallas_call(
        functools.partial(kernel, nz),
        grid=(1,),
        out_shape=(
            jax.ShapeDtypeStruct(queries.shape, BF16),
            jax.ShapeDtypeStruct(queries.shape, BF16),
            jax.ShapeDtypeStruct(keys.shape, BF16),
            jax.ShapeDtypeStruct(keys.shape, BF16),
        ),
        in_specs=[
            pl.BlockSpec((8, entries), lambda i: (rows // 8 - 1, 0), memory_space=pltpu.SMEM),
            any_spec,
            whole,
            whole,
            any_spec,
        ],
        out_specs=[any_spec] * 4,
        scratch_shapes=[
            vm(tok, width),
            vm(tok, width),
            vm(2, part_tok, feat),
            vm(nz + 1, 2, PLANE, blk, width),
            vm(nz + 1, 2, PLANE, blk, width, dtype=F32),
            vm(heads, tok, HD, dtype=F32),
            vm(heads, tok, HD, dtype=F32),
            vm(heads, tok, HD, dtype=F32),
            vm(heads, 8, tok, dtype=F32),
            vm(heads, 8, tok, dtype=F32),
            vm(heads, HD, tok, dtype=F32),
            vm(tok, width),
            vm(tok, width),
            vm(2, blocks, blk, width),
            vm(nz, 2, blk, width),
            vm(nz, 2, 2, blk, width),
            vm(nz, blk, width),
            vm(nz, 4, blk, width),
            vm(nz, 2, half, width),
            vm(nz, 2, blk, width),
            vm(nz, 2, blk, width),
            vm(nz, 2, blk, width),
            vm(nz, 2, 2, blk, width),
            vm(nz, blk, width),
            vm(nz, 4, blk, width),
            vm(nz, 2, half, width),
            vm(nz, 2, blk, width),
            vm(nz, 2, blk, width),
            vm(2, blk, width, dtype=F32),
            dma((2,)),
            dma((n_kv,)),
            dma((n_kv,)),
            dma((2, n_kv)),
            dma((2, n_kv)),
            dma((nz,)),
            dma((nz,)),
            dma((nz, 13)),
            dma((nz, 14)),
            dma((nz, 10)),
            dma((nz, 10)),
            dma((nz,)),
            dma((nz,)),
            dma((n_kv,)),
            dma((n_kv,)),
            dma((n_kv,)),
            dma((n_kv,)),
            dma((2, n_kv)),
            dma((2, n_kv)),
            dma((7,)),
        ],
        compiler_params=pltpu.CompilerParams(
            collective_id=0, has_side_effects=True, vmem_limit_bytes=58 * 1024 * 1024
        ),
    )(layout, queries, keys, values, grad_out)


def solution(mesh):
    return jax.shard_map(
        shards,
        mesh=mesh,
        in_specs=(P("seq", None), P("seq", "kv", None), P("seq", "kv", None), P(), P("seq", None)),
        out_specs=(P("seq", None), P("seq", None), P("seq", "kv", None), P("seq", "kv", None)),
        check_vma=False,
    )
```

time: 1230 us -> 132 us (0.11)
  the two profiles are of different devices: /device:TPU:16 before, /device:TPU:225 now
where the time goes in v1:
time: 132 us
  Pallas kernels  124 us (94%)
  local copies, waits for them, and re-layouts  6.94 us (5%)
    pallas_call x1, Pallas kernels, shards(): pl.pallas_call(functools.partial(kernel, nz), grid=(1,), out_shape=(jax.S...  124 us
    unnamed x11, local copies, waits for them, and re-layouts  6.94 us

profile of v1, /device:TPU:225, one launch (start us, length us, event | category | flops | bytes accessed | tf_op | source)
XLA Modules:
  0.0 132.0 jit_solution(15097585878263531842)
XLA Ops:
  0.6 1.8 %copy.9.layout_ref = s32[512,71]{1,0:T(8,128)} copy(s32[512,71]{0,1:T(8,128)} %param.8) | data formatting | bytes 290816 | tf_op args[3]
  2.4 124.5 %shard_map.84 = (bf16[512,1024]{1,0:T(8,128)(2,1)}, bf16[512,1024]{1,0:T(8,128)(2,1)}, bf16[8,16,1024]{2,1,0:T(8,128)(2,1)}, bf16[8,16,1024]{2,1,0:T(8,128)(2,1)}) custom-call(s32[512,71]{1,0:T(8,128)} %copy.9.layout_ref, bf16[512,1024]{1,0:T(8,128)(2,1)} %q_hbm.1, bf16[8,16,1024]{2,1,0:T(8,128)(2,1)} %k_in.1, bf16[8,16,1024]{2,1,0:T(8,128)(2,1)} %v_in.1, ...), custom_call_target="tpu_custom_call" | custom-call | tf_op jit(solution)/shard_map/pallas_call | solution.py:502
  126.8 0.0 copy-start
  126.8 2.4 %copy.14 = bf16[512,1024]{1,0:T(8,128)(2,1)} copy(bf16[512,1024]{1,0:T(8,128)(2,1)} %get-tuple-element.8) | data formatting | bytes 2097152
  129.2 0.0 copy-done
  129.2 0.0 copy-start.2
  129.2 1.0 copy.15
  130.2 0.1 copy-done.2
  130.3 0.0 copy-start.1
  130.3 0.7 copy.16
  131.0 0.3 copy-done.1
  131.3 0.7 copy.17
Async XLA Ops:
  126.8 2.4 %copy-start = (bf16[512,1024]{1,0:T(8,128)(2,1)S(1)}, bf16[512,1024]{1,0:T(8,128)(2,1)}, u32[]{:S(2)}) copy-start(bf16[512,1024]{1,0:T(8,128)(2,1)} %get-tuple-element.9) | copy-start | bytes 3145732
  129.2 1.1 copy-start.2
  130.3 1.0 copy-start.1

commit v2 on v0

v2 whole, which is shorter than its diff:
```python
import functools
import math

import jax
import jax.numpy as jnp
from jax import lax
from jax.experimental import pallas as pl
from jax.experimental.pallas import tpu as pltpu
from jax.sharding import PartitionSpec as P

HD = 128
PLANE = 8
MESH = pl.DeviceIdType.MESH
F32 = jnp.float32
BF16 = jnp.bfloat16
SCALE = 1.0 / math.sqrt(HD)
LOG2_SCALE = math.log2(math.e) / math.sqrt(HD)
NT = (((1,), (1,)), ((), ()))
NN = (((1,), (0,)), ((), ()))
TN = (((0,), (0,)), ((), ()))
KEY_TILE = 256
LAG = 2
VMEM_LIMIT = 123 * 512 * 1024


def dot(a, b, dims):
    return lax.dot_general(a, b, dims, preferred_element_type=F32)


def kernel(
    nz, layout_hbm, q_hbm, k_hbm, v_hbm, do_hbm,
    att_out, dq_out, dk_out, dv_out,
    lay, k_in, v_in, q, do, sums, ag, grad, m, l, acc, lse_row, delta_row, dqt, att, dq, fin, fin_in, tail, tail_in, res,
    s0, s1, s2, s3, sz, szl, r0, r1, r2, r3, rz, rzl, own,
    load_sem, sum_s, sum_r, kv_s, kv_r, zs, zr, zl_s, zl_r, ag_s, ag_r, rs_s, rs_r, gz_s, gz_r,
    gl_s, gl_r, att_s, att_r, dq_s, dq_r, fin_s, fin_r, tail_s, tail_r, first_s, first_r, d0_s, d0_r, loc_sem,
):
    heads, tok, _ = q.shape
    width = heads * HD
    blocks, part_tok = k_in.shape[0], k_in.shape[1]
    blk = ag.shape[4]
    n_kv = lax.axis_size("kv")
    s = lax.axis_index("seq")
    k = lax.axis_index("kv")
    z, r = s // PLANE, s % PLANE
    x, y = r // 2, r % 2
    left, right, opp, yo = (x + 3) % 4, (x + 1) % 4, (x + 2) % 4, 1 - y
    base = z * PLANE
    dev_left = {"seq": base + left * 2 + y}
    dev_right = {"seq": base + right * 2 + y}
    dev_y = {"seq": base + x * 2 + yo}
    dev_up = {"seq": s + PLANE}
    dev_down = {"seq": s - PLANE}
    dev_top = {"seq": (nz - 1) * PLANE + r}
    dev_bottom = {"seq": r}
    has_up, has_down = z + 1 < nz, z > 0
    wrap = nz > 2
    is_bottom, is_top = z == 0, z == nz - 1
    peers = [(k + i) % n_kv for i in range(1, n_kv)]
    sibling = (k // 2) * 2 + (k + 1) % 2
    across = (k + 2) % n_kv
    corner = (sibling + 2) % n_kv
    far = jnp.maximum(0, jnp.minimum(z, nz - 2) - 1)
    done = 3 * LAG - 1
    ends = [far + done, jnp.maximum(2 * far + done, far + done + 1)]
    bwd_at = ends[0] + 1

    def peer_cols(p):
        return pl.ds(pl.multiple_of(p * width, width), width)

    cols = peer_cols(k)

    def head_cols(p, h):
        return pl.ds(pl.multiple_of(p * width + h * HD, HD), HD)

    def part(p):
        return pl.ds(pl.multiple_of(p * part_tok, part_tok), part_tok)

    def rcopy(src, dst, send, recv, dev):
        return pltpu.make_async_remote_copy(
            src_ref=src, dst_ref=dst, send_sem=send, recv_sem=recv, device_id=dev, device_id_type=MESH
        )

    barrier = pltpu.get_barrier_semaphore()
    for p in peers:
        pl.semaphore_signal(barrier, inc=1, device_id={"kv": p}, device_id_type=MESH)
    mates = [(r + i) % PLANE for i in range(1, PLANE)]
    for w in mates:
        pl.semaphore_signal(barrier, inc=1, device_id={"seq": base + w}, device_id_type=MESH)
    for i in range(1, nz):
        pl.semaphore_signal(
            barrier, inc=1, device_id={"seq": ((z + i) % nz) * PLANE + r}, device_id_type=MESH
        )
    loads = [
        pltpu.make_async_copy(src, dst, load_sem.at[i])
        for i, (src, dst) in enumerate(
            (
                (layout_hbm.at[:, pl.ds(layout_hbm.shape[1] - lay.shape[1], lay.shape[1])], lay),
                (k_hbm, k_in),
                (v_hbm, v_in),
                *((q_hbm.at[:, head_cols(k, h)], q.at[h]) for h in range(heads)),
                *((do_hbm.at[:, head_cols(k, h)], do.at[h]) for h in range(heads)),
            )
        )
    ]
    for c in loads:
        c.start()
    for c in loads[:3]:
        c.wait()
    entry = lax.broadcasted_iota(jnp.int32, (lay.shape[0], 1), 0)
    last_row = lay[:, lay.shape[1] - 1 :]
    named = jnp.where(entry == jnp.minimum(s, nz * PLANE - 2), last_row, 0)
    summary = jnp.clip(jnp.sum(named, axis=0, keepdims=True) - s * blocks, 0, blocks - 1)
    for t, ref in enumerate((k_in, v_in)):
        picked = ref[0]
        for b in range(1, blocks):
            picked = jnp.where(summary == b, ref[b], picked)
        for h in range(n_kv * heads):
            sums[h, t] = picked[:, h * HD : h * HD + HD]
    pl.semaphore_wait(barrier, len(peers) + PLANE - 1 + nz - 1)

    def sum_copy(p, slot):
        return rcopy(
            sums.at[pl.ds(p * heads, heads)],
            ag.at[z, :, :, r, part(slot)],
            sum_s.at[p],
            sum_r.at[slot],
            {"kv": p},
        )

    for p in peers:
        sum_copy(p, k).start()
    own_sum = pltpu.make_async_copy(
        sums.at[pl.ds(k * heads, heads)], ag.at[z, :, :, r, part(k)], loc_sem.at[0]
    )
    own_sum.start()

    def kv_copies(p, slot):
        return [
            rcopy(
                ref.at[:, :, head_cols(p, h)],
                ag.at[nz, h, t, :, part(slot)],
                kv_s.at[h, t, p],
                kv_r.at[h, t, slot],
                {"kv": p},
            )
            for h in range(heads)
            for t, ref in enumerate((k_in, v_in))
        ]

    own_kv = [
        pltpu.make_async_copy(
            ref.at[:, :, head_cols(k, h)], ag.at[nz, h, t, :, part(k)], loc_sem.at[1 + 2 * h + t]
        )
        for h in range(heads)
        for t, ref in enumerate((k_in, v_in))
    ]
    for c in own_kv:
        c.start()
    own_sum.wait()
    for p in peers:
        sum_copy(p, p).wait_recv()


    def agc(o, h, i, ref, dev):
        return rcopy(ref, ref, ag_s.at[o, h, i], ag_r.at[o, h, i], dev)

    def block(o, h, xx, yy):
        return ag.at[o, h, :, xx * 2 + yy]

    def pair(o, h, xx):
        return ag.at[o, h, :, pl.ds(xx * 2, 2)]

    def pair_of(o, h, t, xx):
        return ag.at[o, h, t, pl.ds(xx * 2, 2)]

    def ag1(o, h):
        return [agc(o, h, 0, block(o, h, x, y), dev_y)]

    def ag1_in(o, h):
        return [agc(o, h, 0, block(o, h, x, yo), dev_y)]

    def ag2(o, h):
        return [agc(o, h, 1, pair(o, h, x), dev_right), agc(o, h, 2, pair(o, h, x), dev_left)]

    def ag2_in(o, h):
        return [agc(o, h, 1, pair(o, h, left), dev_left), agc(o, h, 2, pair(o, h, right), dev_right)]

    def ag3(o, h):
        return [
            agc(o, h, 3, pair_of(o, h, 0, left), dev_right),
            agc(o, h, 4, pair_of(o, h, 1, right), dev_left),
        ]

    def ag3_in(o, h):
        return [
            agc(o, h, 3, pair_of(o, h, 0, opp), dev_left),
            agc(o, h, 4, pair_of(o, h, 1, opp), dev_right),
        ]

    def start(copies):
        for c in copies:
            c.start()

    def recv(copies):
        for c in copies:
            c.wait_recv()

    def sent(copies):
        for c in copies:
            c.wait_send()

    def z_copy(dz, h):
        return rcopy(ag.at[z, h, :, r], ag.at[z, h, :, r], zs.at[dz, h], zr.at[z, h], {"seq": s + dz * PLANE})

    def up_copy(o, h):
        return rcopy(ag.at[o, h], ag.at[o, h], zl_s.at[0, h], zl_r.at[0, h], dev_up)

    def wrap_copy(o, h):
        return rcopy(ag.at[o, h], ag.at[o, h], zl_s.at[1, h], zl_r.at[1, h], dev_top)

    def first_copy(w, slot):
        ref = ag.at[z, :, :, slot]
        return rcopy(ref, ref, first_s.at[w], first_r.at[slot], {"seq": base + w})

    for w in mates:
        first_copy(w, r).start()
    for h in range(heads):
        for dz in range(2, nz - 1):
            @pl.when(z + dz < nz)
            def _(dz=dz, h=h):
                z_copy(dz, h).start()

    for p in peers:
        start(kv_copies(p, k))
    m[...] = jnp.full_like(m, -1e30)
    l[...] = jnp.zeros_like(l)
    acc[...] = jnp.zeros_like(acc)
    dqt[...] = jnp.zeros_like(dqt)
    for c in loads[3:]:
        c.wait()
    for w in mates:
        first_copy(w, w).wait_recv()
    for h in range(heads):
        @pl.when(has_up)
        def _(h=h):
            up_copy(z, h).start()

        if wrap:
            @pl.when(is_bottom)
            def _(h=h):
                wrap_copy(z, h).start()

    plane_keys = PLANE * blk

    def forward(c, h, slope, offset, masked):
        kk = ag[c, h, 0].reshape(plane_keys, HD)
        vv = ag[c, h, 1].reshape(plane_keys, HD)
        score = dot(q[h], kk, NT) * LOG2_SCALE
        tiles = [score[:, j * HD : j * HD + HD] for j in range(plane_keys // HD)]
        if masked:
            row = lax.broadcasted_iota(jnp.int32, (tok, 1), 0) * slope + offset
            lane = lax.broadcasted_iota(jnp.int32, (tok, HD), 1)
            tiles = [jnp.where(lane + j * HD <= row, t, -jnp.inf) for j, t in enumerate(tiles)]
        top = functools.reduce(jnp.maximum, tiles)
        m_old = m[h]
        m_new = jnp.maximum(m_old, jnp.max(top, axis=1, keepdims=True))
        alpha = jnp.exp2(m_old - m_new)
        weights = [jnp.exp2(t - m_new) for t in tiles]
        l[h] = l[h] * alpha + functools.reduce(jnp.add, weights)
        w = jnp.concatenate([t.astype(BF16) for t in weights], axis=1)
        acc[h] = acc[h] * alpha + dot(w, vv, NN)
        m[h] = m_new

    def out_copy(src, dst, send, recv_, i, p, slot, h):
        return rcopy(
            src.at[h], dst.at[:, head_cols(slot, h)], send.at[i, h], recv_.at[i, h], {"kv": p}
        )

    def pass_on(dst, send, recv_, slot, h):
        ref = dst.at[:, head_cols(slot, h)]
        return rcopy(ref, ref, send.at[2, h], recv_.at[2, h], {"kv": sibling})

    def out_own(src, dst, i, h):
        return pltpu.make_async_copy(src.at[h], dst.at[:, head_cols(k, h)], loc_sem.at[i + h])

    def out_start(src, dst, send, recv_, i, h):
        out_copy(src, dst, send, recv_, 1, across, k, h).start()
        out_copy(src, dst, send, recv_, 0, sibling, k, h).start()
        out_own(src, dst, i, h).start()

    def out_forward(src, dst, send, recv_, i, h):
        out_copy(src, dst, send, recv_, 1, across, across, h).wait_recv()
        pass_on(dst, send, recv_, across, h).start()

    def out_finish(src, dst, send, recv_, i, h):
        out_own(src, dst, i, h).wait()
        out_copy(src, dst, send, recv_, 0, sibling, sibling, h).wait_recv()
        pass_on(dst, send, recv_, corner, h).wait_recv()
        for slot, p in ((0, sibling), (1, across)):
            out_copy(src, dst, send, recv_, slot, p, k, h).wait_send()
        pass_on(dst, send, recv_, across, h).wait_send()

    att_args = (att, att_out, att_s, att_r, 5)
    dq_args = (dq, dq_out, dq_s, dq_r, 7)

    def far_unit(u):
        h = jnp.where(u >= far, 1, 0)
        return z - (2 + u - h * far), h

    over_at = [jnp.minimum(done + 2, ends[0]), jnp.minimum(done + 3, ends[1])]

    def fwd_step(it):
        @pl.when(it < 2 * far)
        def _():
            o, h = far_unit(it)
            rcopy(ag.at[o, h, :, r], ag.at[o, h, :, r], zs.at[0, h], zr.at[o, h], dev_y).wait_recv()
            start(ag1(o, h))

        @pl.when((it >= LAG) & (it - LAG < 2 * far))
        def _():
            o, h = far_unit(it - LAG)
            recv(ag1_in(o, h))
            start(ag2(o, h))

        @pl.when((it >= 2 * LAG) & (it - 2 * LAG < 2 * far))
        def _():
            o, h = far_unit(it - 2 * LAG)
            recv(ag2_in(o, h))
            start(ag3(o, h))

        @pl.when(it < 4)
        def _():
            local = it % 2 == 1

            @pl.when(it == 1)
            def _():
                for c in own_kv:
                    c.wait()
                for p in peers:
                    recv(kv_copies(p, p))

            forward(
                jnp.where(local, nz, z),
                it // 2,
                jnp.where(local, 1, 0),
                jnp.where(local, 0, r * blk - 1),
                True,
            )

        def chunk(j, _):
            o, h = far_unit(it - 3 * LAG)
            inner = (j == 0) & (it >= 3 * LAG) & (it - 3 * LAG < 2 * far)
            second = jnp.where(j == 1, jnp.where(it == done + 1, 1, 0), jnp.where(it == over_at[1], 1, 0))
            below = (j == 1) & ((it == done) | (it == done + 1)) & has_down
            over = (j == 2) & ((it == over_at[0]) | (it == over_at[1])) & is_top & wrap

            @pl.when(inner)
            def _():
                recv(ag3_in(o, h))

            @pl.when(below)
            def _():
                up_copy(z - 1, second).wait_recv()

            if wrap:
                @pl.when(over)
                def _():
                    wrap_copy(0, second).wait_recv()

            @pl.when(inner | below | over)
            def _():
                forward(
                    jnp.where(j == 0, o, jnp.where(j == 1, z - 1, 0)), jnp.where(j == 0, h, second), 0, 0, False
                )

            return 0

        lax.fori_loop(0, 3, chunk, 0)

        @pl.when((it == ends[0]) | (it == ends[1]))
        def _():
            h = jnp.where(it == ends[1], 1, 0)
            total = jnp.sum(l[h], axis=1, keepdims=True)
            out = (acc[h] / total).astype(BF16)
            att[h] = out
            delta = jnp.sum(out.astype(F32) * do[h].astype(F32), axis=1, keepdims=True)
            lse_row[h] = jnp.transpose(m[h] + jnp.log2(total))[:8]
            delta_row[h] = jnp.transpose(jnp.broadcast_to(delta, (tok, HD)))[:8]
            out_start(*att_args, h)

    def backward(c, h, slope, offset, masked):
        tile_blocks = KEY_TILE // blk
        lse = lse_row[h, 0:1, :]
        delta = delta_row[h, 0:1, :]
        qh, doh = q[h], do[h]
        for t in range(plane_keys // KEY_TILE):
            bs = slice(t * tile_blocks, (t + 1) * tile_blocks)
            kk = ag[c, h, 0, bs].reshape(KEY_TILE, HD)
            vv = ag[c, h, 1, bs].reshape(KEY_TILE, HD)
            prob = jnp.exp2(dot(kk, qh, NT) * LOG2_SCALE - lse)
            if masked:
                row = lax.broadcasted_iota(jnp.int32, (1, tok), 1) * slope + offset
                key = lax.broadcasted_iota(jnp.int32, (KEY_TILE, tok), 0) + t * KEY_TILE
                prob = jnp.where(key <= row, prob, 0.0)
            ds = (prob * (dot(vv, doh, NT) - delta)).astype(BF16)
            grad[c, h, 1, bs] = dot(prob.astype(BF16), doh, NN).reshape(tile_blocks, blk, HD)
            grad[c, h, 0, bs] = (dot(ds, qh, NN) * SCALE).reshape(tile_blocks, blk, HD)
            dqt[h] += dot(kk, ds, TN)

    def rsc(o, h, i, src, dst, dev):
        return rcopy(src, dst, rs_s.at[o, h, i], rs_r.at[o, h, i], dev)

    def rs1(o, h):
        return [
            rsc(o, h, 0, s1.at[o, h, 0], r1.at[o, h, 0], dev_left),
            rsc(o, h, 1, s1.at[o, h, 1], r1.at[o, h, 1], dev_right),
        ]

    def rs2(o, h):
        return [
            rsc(o, h, 2, s2.at[o, h, 0], r2.at[o, h, 0], dev_left),
            rsc(o, h, 3, s2.at[o, h, 1], r2.at[o, h, 1], dev_right),
        ]

    def rs3(o, h):
        return [rsc(o, h, 4, s3.at[o, h], r3.at[o, h], dev_y)]

    def gz_copy(o, h):
        return rcopy(sz.at[o, h], rz.at[z, h], gz_s.at[o, h], gz_r.at[z, h], {"seq": o * PLANE + r})

    def down_copy(h):
        return rcopy(szl.at[0, h], rzl.at[0, h], gl_s.at[0, h], gl_r.at[0, h], dev_down)

    def around_copy(h):
        return rcopy(szl.at[1, h], rzl.at[1, h], gl_s.at[1, h], gl_r.at[1, h], dev_bottom)

    def two(xx):
        return pl.ds(xx * 2, 2)

    def reduce1(o, h):
        s1[o, h, 0] = grad[o, h, 0, two(opp)].astype(BF16)
        s1[o, h, 1] = grad[o, h, 1, two(opp)].astype(BF16)
        start(rs1(o, h))

    def reduce2(o, h):
        recv(rs1(o, h))
        s2[o, h, 0, 0] = (grad[o, h, 0, two(left)] + r1[o, h, 0].astype(F32)).astype(BF16)
        s2[o, h, 0, 1] = grad[o, h, 1, two(left)].astype(BF16)
        s2[o, h, 1, 0] = grad[o, h, 0, two(right)].astype(BF16)
        s2[o, h, 1, 1] = (grad[o, h, 1, two(right)] + r1[o, h, 1].astype(F32)).astype(BF16)
        start(rs2(o, h))

    def summed(o, h, t, yy):
        return grad[o, h, t, x * 2 + yy] + (r2[o, h, 0, t, yy].astype(F32) + r2[o, h, 1, t, yy].astype(F32))

    def reduce3(o, h):
        recv(rs2(o, h))
        for t in range(2):
            s3[o, h, t] = summed(o, h, t, yo).astype(BF16)
        start(rs3(o, h))

    def reduce4(o, h):
        recv(rs3(o, h))
        for t in range(2):
            sz[o, h, t] = (summed(o, h, t, y) + r3[o, h, t].astype(F32)).astype(BF16)
        gz_copy(o, h).start()

    def d0_copy(w, slot, h):
        return rcopy(s0.at[h, w], r0.at[h, slot], d0_s.at[h, w], d0_r.at[h, slot], {"seq": base + w})

    def fin_copy(h, t, p, slot):
        return rcopy(
            fin.at[h, t, :, part(p)],
            fin_in.at[t, :, :, head_cols(slot, h)],
            fin_s.at[h, t, p],
            fin_r.at[h, t, slot],
            {"kv": p},
        )

    def own_fin(h, t):
        return pltpu.make_async_copy(
            fin.at[h, t, :, part(k)], fin_in.at[t, :, :, head_cols(k, h)], loc_sem.at[9 + 2 * h + t]
        )

    def far_grad(g):
        h = jnp.where(g >= z, 1, 0)
        j = g - h * z
        return jnp.where(j == 0, z - 1, j - 1), h, j

    def in_plane(g):
        _, _, j = far_grad(g)
        whole = j == 0
        if wrap:
            whole = whole | ((j == 1) & is_top)
        return (g >= 0) & (g < 2 * z) & jnp.logical_not(whole)

    def bwd_step(g):
        o, h, j = far_grad(g)

        @pl.when(g < 2 * z)
        def _():
            backward(o, h, 0, 0, False)

            @pl.when(j == 0)
            def _():
                szl[0, h] = grad[z - 1, h].astype(BF16)
                down_copy(h).start()

            if wrap:
                @pl.when((j == 1) & is_top)
                def _():
                    szl[1, h] = grad[0, h].astype(BF16)
                    around_copy(h).start()

        @pl.when(in_plane(g))
        def _():
            reduce1(o, h)

        @pl.when((g >= 2 * z) & (g < 2 * z + 4))
        def _():
            n = g - 2 * z
            head, local = n // 2, n % 2 == 1
            backward(
                jnp.where(local, nz, z), head, jnp.where(local, 1, 0), jnp.where(local, 0, r * blk - 1), True
            )

            @pl.when(local)
            def _():
                dq[head] = jnp.transpose(dqt[head] * SCALE).astype(BF16)
                out_start(*dq_args, head)
                fin[head] = grad[nz, head].astype(BF16)
                for t in range(2):
                    own_fin(head, t).start()
                    for p in peers:
                        fin_copy(head, t, p, k).start()

            @pl.when(jnp.logical_not(local))
            def _():
                @pl.when(has_up)
                def _():
                    down_copy(head).wait_recv()
                    grad[z, head] += rzl[0, head].astype(F32)

                if wrap:
                    @pl.when(is_bottom)
                    def _():
                        around_copy(head).wait_recv()
                        grad[z, head] += rzl[1, head].astype(F32)

                for w in range(PLANE):
                    for t in range(2):
                        s0[head, w, t] = grad[z, head, t, w].astype(BF16)
                for w in mates:
                    d0_copy(w, r, head).start()

        for back, stage in ((3, reduce4), (2, reduce3), (1, reduce2)):
            @pl.when(in_plane(g - back * LAG))
            def _(back=back, stage=stage):
                stage(*far_grad(g - back * LAG)[:2])

    last_it = bwd_at + 2 * z + 3 * LAG - 1

    def step(it, _):
        @pl.when(it <= ends[1])
        def _():
            fwd_step(it)

        @pl.when(it >= bwd_at)
        def _():
            bwd_step(it - bwd_at)

        for h in range(heads):
            @pl.when(it == ends[h] + 4)
            def _(h=h):
                out_forward(*att_args, h)

        @pl.when(it == last_it)
        def _():
            out_forward(*dq_args, 0)

        return 0

    lax.fori_loop(0, last_it + 1, step, 0)
    out_forward(*dq_args, 1)
    for h in range(heads):
        for w in mates:
            d0_copy(w, w, h).wait_recv()
        for t in range(2):
            own[h, t] = functools.reduce(jnp.add, [r0[h, w, t].astype(F32) for w in mates], grad[z, h, t, r])

    def add_plane(o, _):
        for h in range(heads):
            rcopy(sz.at[0, h], rz.at[o, h], gz_s.at[0, h], gz_r.at[o, h], dev_y).wait_recv()
        own[...] += rz[o].astype(F32)
        return 0

    lax.fori_loop(z + 2, jnp.where(is_bottom, nz - 1, nz), add_plane, 0)
    tail[...] = own[...].astype(BF16)

    def tail_copy(p, slot):
        return rcopy(
            tail.at[:, :, part(p)],
            tail_in.at[pl.ds(slot * heads, heads)],
            tail_s.at[p],
            tail_r.at[slot],
            {"kv": p},
        )

    for p in peers:
        tail_copy(p, k).start()
    own_tail = pltpu.make_async_copy(
        tail.at[:, :, part(k)], tail_in.at[pl.ds(k * heads, heads)], loc_sem.at[13]
    )
    own_tail.start()
    for p in peers:
        sum_copy(p, k).wait_send()
        sent(kv_copies(p, k))
    for w in mates:
        first_copy(w, r).wait_send()

    def sent_head(h, _):
        for dz in range(2, nz - 1):
            @pl.when(z + dz < nz)
            def _(dz=dz):
                z_copy(dz, h).wait_send()

        @pl.when(has_up)
        def _():
            up_copy(z, h).wait_send()

        @pl.when(has_down)
        def _():
            down_copy(h).wait_send()

        if wrap:
            @pl.when(is_bottom)
            def _():
                wrap_copy(z, h).wait_send()

            @pl.when(is_top)
            def _():
                around_copy(h).wait_send()

        def sent_plane(o, _):
            direct = (o + 1 != z) & jnp.logical_not((o == 0) & is_top)

            @pl.when(direct)
            def _():
                sent(ag1(o, h) + ag2(o, h) + ag3(o, h) + rs1(o, h) + rs2(o, h) + rs3(o, h))
                gz_copy(o, h).wait_send()

            return 0

        for w in mates:
            d0_copy(w, r, h).wait_send()
        lax.fori_loop(0, z, sent_plane, 0)
        return 0

    lax.fori_loop(0, heads, sent_head, 0)
    for h in range(heads):
        out_finish(*att_args, h)
        out_finish(*dq_args, h)
    for h in range(heads):
        for t in range(2):
            own_fin(h, t).wait()
            for p in peers:
                fin_copy(h, t, p, p).wait_recv()
    own_tail.wait()
    for p in peers:
        tail_copy(p, p).wait_recv()
    results = [
        pltpu.make_async_copy(res.at[t], ref, loc_sem.at[14 + t]) for t, ref in enumerate((dk_out, dv_out))
    ]
    for t in range(2):
        arrived = jnp.concatenate([tail_in[h, t].astype(F32) for h in range(n_kv * heads)], axis=1)
        for b in range(blocks):
            res[t, b] = (fin_in[t, b].astype(F32) + jnp.where(summary == b, arrived, 0.0)).astype(BF16)
        results[t].start()

    for p in peers:
        tail_copy(p, k).wait_send()
        for h in range(heads):
            for t in range(2):
                fin_copy(h, t, p, k).wait_send()
    for c in results:
        c.wait()


def hand_over(*refs):
    n = (len(refs) - 2) // 3
    ins, outs, held = refs[:n], refs[n : 2 * n], refs[2 * n : 3 * n]
    load_sem, save_sem = refs[3 * n :]
    loads = [pltpu.make_async_copy(a, b, load_sem.at[i]) for i, (a, b) in enumerate(zip(ins, held))]
    saves = [pltpu.make_async_copy(a, b, save_sem.at[i]) for i, (a, b) in enumerate(zip(held, outs))]
    for c in loads:
        c.start()
    for load, save in zip(loads, saves):
        load.wait()
        save.start()
    for c in saves:
        c.wait()


def shards(queries, keys, values, layout, grad_out):
    tok, feat = queries.shape
    blocks, part_tok = keys.shape[0], keys.shape[1]
    n_kv = lax.axis_size("kv")
    nz = lax.axis_size("seq") // PLANE
    blk = part_tok * n_kv
    width = feat // n_kv
    heads = width // HD
    dma = pltpu.SemaphoreType.DMA

    def vm(*shape, dtype=BF16):
        return pltpu.VMEM(shape, dtype)

    results = tuple(jax.ShapeDtypeStruct(a.shape, BF16) for a in (queries, queries, keys, keys))
    hbm = [pl.BlockSpec(memory_space=pltpu.HBM)]
    made = pl.pallas_call(
        functools.partial(kernel, nz),
        out_shape=results,
        in_specs=hbm * 5,
        out_specs=hbm * 4,
        scratch_shapes=[
            vm(layout.shape[1], min(128, layout.shape[0]), dtype=jnp.int32),
            vm(*keys.shape),
            vm(*keys.shape),
            vm(heads, tok, HD),
            vm(heads, tok, HD),
            vm(n_kv * heads, 2, part_tok, HD),
            vm(nz + 1, heads, 2, PLANE, blk, HD),
            vm(nz + 1, heads, 2, PLANE, blk, HD, dtype=F32),
            vm(heads, tok, HD, dtype=F32),
            vm(heads, tok, HD, dtype=F32),
            vm(heads, tok, HD, dtype=F32),
            vm(heads, 8, tok, dtype=F32),
            vm(heads, 8, tok, dtype=F32),
            vm(heads, HD, tok, dtype=F32),
            vm(heads, tok, HD),
            vm(heads, tok, HD),
            vm(heads, 2, blocks, blk, HD),
            vm(2, blocks, part_tok, feat),
            vm(heads, 2, blk, HD),
            vm(n_kv * heads, 2, part_tok, HD),
            vm(2, blocks, part_tok, feat),
            vm(heads, PLANE, 2, blk, HD),
            vm(nz, heads, 2, 2, blk, HD),
            vm(nz, heads, 2, 2, 2, blk, HD),
            vm(nz, heads, 2, blk, HD),
            vm(nz, heads, 2, blk, HD),
            vm(2, heads, 2, PLANE, blk, HD),
            vm(heads, PLANE, 2, blk, HD),
            vm(nz, heads, 2, 2, blk, HD),
            vm(nz, heads, 2, 2, 2, blk, HD),
            vm(nz, heads, 2, blk, HD),
            vm(nz, heads, 2, blk, HD),
            vm(2, heads, 2, PLANE, blk, HD),
            vm(heads, 2, blk, HD, dtype=F32),
            dma((3 + 2 * heads,)),
            dma((n_kv,)),
            dma((n_kv,)),
            dma((heads, 2, n_kv)),
            dma((heads, 2, n_kv)),
            dma((nz, heads)),
            dma((nz, heads)),
            dma((2, heads)),
            dma((2, heads)),
            dma((nz, heads, 5)),
            dma((nz, heads, 5)),
            dma((nz, heads, 5)),
            dma((nz, heads, 5)),
            dma((nz, heads)),
            dma((nz, heads)),
            dma((2, heads)),
            dma((2, heads)),
            dma((3, heads)),
            dma((3, heads)),
            dma((3, heads)),
            dma((3, heads)),
            dma((heads, 2, n_kv)),
            dma((heads, 2, n_kv)),
            dma((n_kv,)),
            dma((n_kv,)),
            dma((PLANE,)),
            dma((PLANE,)),
            dma((heads, PLANE)),
            dma((heads, PLANE)),
            dma((16,)),
        ],
        compiler_params=pltpu.CompilerParams(
            collective_id=0, has_side_effects=True, vmem_limit_bytes=VMEM_LIMIT
        ),
    )(layout.T, queries, keys, values, grad_out)
    return pl.pallas_call(
        hand_over,
        out_shape=results,
        in_specs=hbm * 4,
        out_specs=hbm * 4,
        scratch_shapes=[*(vm(*a.shape) for a in results), dma((4,)), dma((4,))],
        compiler_params=pltpu.CompilerParams(vmem_limit_bytes=VMEM_LIMIT),
    )(*made)


def solution(mesh):
    return jax.shard_map(
        shards,
        mesh=mesh,
        in_specs=(P("seq", None), P("seq", "kv", None), P("seq", "kv", None), P(), P("seq", None)),
        out_specs=(P("seq", None), P("seq", None), P("seq", "kv", None), P("seq", "kv", None)),
        check_vma=False,
    )
```

time: 1230 us -> 107 us (0.09)
  the two profiles are of different devices: /device:TPU:16 before, /device:TPU:161 now
where the time goes in v2:
time: 107 us
  Pallas kernels  107 us (100%)
    pallas_call x1, Pallas kernels, shards(): pl.pallas_call(functools.partial(kernel, nz), out_shape=results, in_specs...  104 us
    pallas_call x1, Pallas kernels, shards(): pl.pallas_call(hand_over, out_shape=results, in_specs=hbm * 4, out_specs=...  2.77 us

profile of v2, /device:TPU:161, one launch (start us, length us, event | category | flops | bytes accessed | tf_op | source)
XLA Modules:
  0.0 107.3 jit_solution(2504988373804404225)
XLA Ops:
  0.6 103.9 %shard_map.84 = (bf16[512,1024]{1,0:T(8,128)(2,1)}, bf16[512,1024]{1,0:T(8,128)(2,1)}, bf16[8,16,1024]{2,1,0:T(8,128)(2,1)}, bf16[8,16,1024]{2,1,0:T(8,128)(2,1)}) custom-call(s32[71,512]{1,0:T(8,128)} %bitcast.1, bf16[512,1024]{1,0:T(8,128)(2,1)} %q_hbm.1, bf16[8,16,1024]{2,1,0:T(8,128)(2,1)} %k_hbm.1, bf16[8,16,1024]{2,1,0:T(8,128)(2,1)} %v_hbm.1, ...), custom_call_target="tpu_custom_call" | custom-call | tf_op jit(solution)/shard_map/pallas_call | solution.py:720
  104.5 2.8 %shard_map.85 = (bf16[512,1024]{1,0:T(8,128)(2,1)}, bf16[512,1024]{1,0:T(8,128)(2,1)}, bf16[8,16,1024]{2,1,0:T(8,128)(2,1)}, bf16[8,16,1024]{2,1,0:T(8,128)(2,1)}) custom-call(bf16[512,1024]{1,0:T(8,128)(2,1)} %get-tuple-element.8.refs_0_, bf16[512,1024]{1,0:T(8,128)(2,1)} %get-tuple-element.9.refs_1_, bf16[8,16,1024]{2,1,0:T(8,128)(2,1)} %get-tuple-element.10.refs_2_, ...), custom_call_target="tpu_custom_call" | custom-call | tf_op jit(solution)/shard_map/pallas_call | solution.py:795

commit v3 on v2

--- a/solution.py
+++ b/solution.py
@@ -33,7 +33,7 @@
     lay, k_in, v_in, q, do, sums, ag, grad, m, l, acc, lse_row, delta_row, dqt, att, dq, fin, fin_in, tail, tail_in, res,
     s0, s1, s2, s3, sz, szl, r0, r1, r2, r3, rz, rzl, own,
     load_sem, sum_s, sum_r, kv_s, kv_r, zs, zr, zl_s, zl_r, ag_s, ag_r, rs_s, rs_r, gz_s, gz_r,
-    gl_s, gl_r, att_s, att_r, dq_s, dq_r, fin_s, fin_r, tail_s, tail_r, first_s, first_r, d0_s, d0_r, loc_sem,
+    gl_s, gl_r, att_s, att_r, dq_s, dq_r, fin_s, fin_r, tail_s, tail_r, d0_s, d0_r, loc_sem,
 ):
     heads, tok, _ = q.shape
     width = heads * HD
@@ -60,7 +60,7 @@
     sibling = (k // 2) * 2 + (k + 1) % 2
     across = (k + 2) % n_kv
     corner = (sibling + 2) % n_kv
-    far = jnp.maximum(0, jnp.minimum(z, nz - 2) - 1)
+    far = jnp.maximum(0, jnp.minimum(z, nz - 2) - 2)
     done = 3 * LAG - 1
     ends = [far + done, jnp.maximum(2 * far + done, far + done + 1)]
     bwd_at = ends[0] + 1
@@ -82,11 +82,10 @@
         )
 
     barrier = pltpu.get_barrier_semaphore()
-    for p in peers:
-        pl.semaphore_signal(barrier, inc=1, device_id={"kv": p}, device_id_type=MESH)
     mates = [(r + i) % PLANE for i in range(1, PLANE)]
-    for w in mates:
-        pl.semaphore_signal(barrier, inc=1, device_id={"seq": base + w}, device_id_type=MESH)
+    around = [(w, p) for w in [r] + mates for p in [k] + peers][1:]
+    for w, p in around:
+        pl.semaphore_signal(barrier, inc=1, device_id={"seq": base + w, "kv": p}, device_id_type=MESH)
     for i in range(1, nz):
         pl.semaphore_signal(
             barrier, inc=1, device_id={"seq": ((z + i) % nz) * PLANE + r}, device_id_type=MESH
@@ -117,19 +116,19 @@
             picked = jnp.where(summary == b, ref[b], picked)
         for h in range(n_kv * heads):
             sums[h, t] = picked[:, h * HD : h * HD + HD]
-    pl.semaphore_wait(barrier, len(peers) + PLANE - 1 + nz - 1)
-
-    def sum_copy(p, slot):
+    pl.semaphore_wait(barrier, len(around) + nz - 1)
+
+    def sum_copy(w, p, from_w, slot):
         return rcopy(
             sums.at[pl.ds(p * heads, heads)],
-            ag.at[z, :, :, r, part(slot)],
-            sum_s.at[p],
-            sum_r.at[slot],
-            {"kv": p},
+            ag.at[z, :, :, from_w, part(slot)],
+            sum_s.at[w, p],
+            sum_r.at[from_w, slot],
+            {"seq": base + w, "kv": p},
         )
 
-    for p in peers:
-        sum_copy(p, k).start()
+    for w, p in around:
+        sum_copy(w, p, r, k).start()
     own_sum = pltpu.make_async_copy(
         sums.at[pl.ds(k * heads, heads)], ag.at[z, :, :, r, part(k)], loc_sem.at[0]
     )
@@ -159,7 +158,7 @@
         c.start()
     own_sum.wait()
     for p in peers:
-        sum_copy(p, p).wait_recv()
+        sum_copy(r, p, r, p).wait_recv()
 
 
     def agc(o, h, i, ref, dev):
@@ -216,17 +215,14 @@
     def up_copy(o, h):
         return rcopy(ag.at[o, h], ag.at[o, h], zl_s.at[0, h], zl_r.at[0, h], dev_up)
 
+    def up2_copy(o, h):
+        return rcopy(ag.at[o, h], ag.at[o, h], zl_s.at[2, h], zl_r.at[2, h], dev_up)
+
     def wrap_copy(o, h):
         return rcopy(ag.at[o, h], ag.at[o, h], zl_s.at[1, h], zl_r.at[1, h], dev_top)
 
-    def first_copy(w, slot):
-        ref = ag.at[z, :, :, slot]
-        return rcopy(ref, ref, first_s.at[w], first_r.at[slot], {"seq": base + w})
-
-    for w in mates:
-        first_copy(w, r).start()
     for h in range(heads):
-        for dz in range(2, nz - 1):
+        for dz in range(3, nz - 1):
             @pl.when(z + dz < nz)
             def _(dz=dz, h=h):
                 z_copy(dz, h).start()
@@ -239,8 +235,8 @@
     dqt[...] = jnp.zeros_like(dqt)
     for c in loads[3:]:
         c.wait()
-    for w in mates:
-        first_copy(w, w).wait_recv()
+    for w, p in around[n_kv - 1 :]:
+        sum_copy(w, p, w, p).wait_recv()
     for h in range(heads):
         @pl.when(has_up)
         def _(h=h):
@@ -306,7 +302,7 @@
 
     def far_unit(u):
         h = jnp.where(u >= far, 1, 0)
-        return z - (2 + u - h * far), h
+        return z - (3 + u - h * far), h
 
     over_at = [jnp.minimum(done + 2, ends[0]), jnp.minimum(done + 3, ends[1])]
 
@@ -348,10 +344,21 @@
                 True,
             )
 
+        @pl.when(((it == done - 1) | (it == done)) & has_down)
+        def _():
+            h = it - (done - 1)
+            up_copy(z - 1, h).wait_recv()
+
+            @pl.when(has_up)
+            def _():
+                up2_copy(z - 1, h).start()
+
         def chunk(j, _):
             o, h = far_unit(it - 3 * LAG)
             inner = (j == 0) & (it >= 3 * LAG) & (it - 3 * LAG < 2 * far)
-            second = jnp.where(j == 1, jnp.where(it == done + 1, 1, 0), jnp.where(it == over_at[1], 1, 0))
+            later = jnp.where(j == 1, done + 1, jnp.where(j == 2, over_at[1], ends[1]))
+            second = jnp.where(it == later, 1, 0)
+            second_below = (j == 3) & ((it == ends[0]) | (it == ends[1])) & (z >= 2)
             below = (j == 1) & ((it == done) | (it == done + 1)) & has_down
             over = (j == 2) & ((it == over_at[0]) | (it == over_at[1])) & is_top & wrap
 
@@ -359,24 +366,24 @@
             def _():
                 recv(ag3_in(o, h))
 
-            @pl.when(below)
-            def _():
-                up_copy(z - 1, second).wait_recv()
+            @pl.when(second_below)
+            def _():
+                up2_copy(z - 2, second).wait_recv()
 
             if wrap:
                 @pl.when(over)
                 def _():
                     wrap_copy(0, second).wait_recv()
 
-            @pl.when(inner | below | over)
+            @pl.when(inner | below | over | second_below)
             def _():
                 forward(
-                    jnp.where(j == 0, o, jnp.where(j == 1, z - 1, 0)), jnp.where(j == 0, h, second), 0, 0, False
+                    jnp.where(j == 0, o, jnp.where(j == 1, z - 1, jnp.where(j == 2, 0, z - 2))), jnp.where(j == 0, h, second), 0, 0, False
                 )
 
             return 0
 
-        lax.fori_loop(0, 3, chunk, 0)
+        lax.fori_loop(0, 4, chunk, 0)
 
         @pl.when((it == ends[0]) | (it == ends[1]))
         def _():
@@ -432,6 +439,9 @@
     def down_copy(h):
         return rcopy(szl.at[0, h], rzl.at[0, h], gl_s.at[0, h], gl_r.at[0, h], dev_down)
 
+    def down2_copy(h):
+        return rcopy(szl.at[2, h], rzl.at[2, h], gl_s.at[2, h], gl_r.at[2, h], dev_down)
+
     def around_copy(h):
         return rcopy(szl.at[1, h], rzl.at[1, h], gl_s.at[1, h], gl_r.at[1, h], dev_bottom)
 
@@ -486,32 +496,40 @@
     def far_grad(g):
         h = jnp.where(g >= z, 1, 0)
         j = g - h * z
-        return jnp.where(j == 0, z - 1, j - 1), h, j
+        next_at = jnp.minimum(z - 1, 4)
+        furthest = j - 1 - jnp.where(j > next_at, 1, 0)
+        return jnp.where(j == next_at, z - 1, jnp.where(j == 0, z - 2, furthest)), h
 
     def in_plane(g):
-        _, _, j = far_grad(g)
-        whole = j == 0
-        if wrap:
-            whole = whole | ((j == 1) & is_top)
-        return (g >= 0) & (g < 2 * z) & jnp.logical_not(whole)
+        o, _ = far_grad(g)
+        return (g >= 0) & (g < 2 * z) & (z - o >= 3) & jnp.logical_not(is_top & (o == 0))
 
     def bwd_step(g):
-        o, h, j = far_grad(g)
+        o, h = far_grad(g)
 
         @pl.when(g < 2 * z)
         def _():
             backward(o, h, 0, 0, False)
 
-            @pl.when(j == 0)
-            def _():
+            @pl.when(o == z - 2)
+            def _():
+                szl[2, h] = grad[o, h].astype(BF16)
+                down2_copy(h).start()
+
+            @pl.when(o == z - 1)
+            def _():
+                @pl.when(has_up)
+                def _():
+                    down2_copy(h).wait_recv()
+                    grad[z - 1, h] += rzl[2, h].astype(F32)
+
                 szl[0, h] = grad[z - 1, h].astype(BF16)
                 down_copy(h).start()
 
-            if wrap:
-                @pl.when((j == 1) & is_top)
-                def _():
-                    szl[1, h] = grad[0, h].astype(BF16)
-                    around_copy(h).start()
+            @pl.when((o == 0) & is_top)
+            def _():
+                szl[1, h] = grad[0, h].astype(BF16)
+                around_copy(h).start()
 
         @pl.when(in_plane(g))
         def _():
@@ -557,7 +575,7 @@
         for back, stage in ((3, reduce4), (2, reduce3), (1, reduce2)):
             @pl.when(in_plane(g - back * LAG))
             def _(back=back, stage=stage):
-                stage(*far_grad(g - back * LAG)[:2])
+                stage(*far_grad(g - back * LAG))
 
     last_it = bwd_at + 2 * z + 3 * LAG - 1
 
@@ -595,7 +613,7 @@
         own[...] += rz[o].astype(F32)
         return 0
 
-    lax.fori_loop(z + 2, jnp.where(is_bottom, nz - 1, nz), add_plane, 0)
+    lax.fori_loop(z + 3, jnp.where(is_bottom, nz - 1, nz), add_plane, 0)
     tail[...] = own[...].astype(BF16)
 
     def tail_copy(p, slot):
@@ -613,14 +631,13 @@
         tail.at[:, :, part(k)], tail_in.at[pl.ds(k * heads, heads)], loc_sem.at[13]
     )
     own_tail.start()
+    for w, p in around:
+        sum_copy(w, p, r, k).wait_send()
     for p in peers:
-        sum_copy(p, k).wait_send()
         sent(kv_copies(p, k))
-    for w in mates:
-        first_copy(w, r).wait_send()
 
     def sent_head(h, _):
-        for dz in range(2, nz - 1):
+        for dz in range(3, nz - 1):
             @pl.when(z + dz < nz)
             def _(dz=dz):
                 z_copy(dz, h).wait_send()
@@ -629,9 +646,17 @@
         def _():
             up_copy(z, h).wait_send()
 
+        @pl.when(has_up & has_down)
+        def _():
+            up2_copy(z - 1, h).wait_send()
+
         @pl.when(has_down)
         def _():
             down_copy(h).wait_send()
+
+        @pl.when(z >= 2)
+        def _():
+            down2_copy(h).wait_send()
 
         if wrap:
             @pl.when(is_bottom)
@@ -643,7 +668,7 @@
                 around_copy(h).wait_send()
 
         def sent_plane(o, _):
-            direct = (o + 1 != z) & jnp.logical_not((o == 0) & is_top)
+            direct = (z - o >= 3) & jnp.logical_not((o == 0) & is_top)
 
             @pl.when(direct)
             def _():
@@ -749,31 +774,31 @@
             vm(nz, heads, 2, 2, 2, blk, HD),
             vm(nz, heads, 2, blk, HD),
             vm(nz, heads, 2, blk, HD),
-            vm(2, heads, 2, PLANE, blk, HD),
+            vm(3, heads, 2, PLANE, blk, HD),
             vm(heads, PLANE, 2, blk, HD),
             vm(nz, heads, 2, 2, blk, HD),
             vm(nz, heads, 2, 2, 2, blk, HD),
             vm(nz, heads, 2, blk, HD),
             vm(nz, heads, 2, blk, HD),
-            vm(2, heads, 2, PLANE, blk, HD),
+            vm(3, heads, 2, PLANE, blk, HD),
             vm(heads, 2, blk, HD, dtype=F32),
             dma((3 + 2 * heads,)),
-            dma((n_kv,)),
-            dma((n_kv,)),
+            dma((PLANE, n_kv)),
+            dma((PLANE, n_kv)),
             dma((heads, 2, n_kv)),
             dma((heads, 2, n_kv)),
             dma((nz, heads)),
             dma((nz, heads)),
-            dma((2, heads)),
-            dma((2, heads)),
+            dma((3, heads)),
+            dma((3, heads)),
             dma((nz, heads, 5)),
             dma((nz, heads, 5)),
             dma((nz, heads, 5)),
             dma((nz, heads, 5)),
             dma((nz, heads)),
             dma((nz, heads)),
-            dma((2, heads)),
-            dma((2, heads)),
+            dma((3, heads)),
+            dma((3, heads)),
             dma((3, heads)),
             dma((3, heads)),
             dma((3, heads)),
@@ -782,8 +807,6 @@
             dma((heads, 2, n_kv)),
             dma((n_kv,)),
             dma((n_kv,)),
-            dma((PLANE,)),
-            dma((PLANE,)),
             dma((heads, PLANE)),
             dma((heads, PLANE)),
             dma((16,)),

time: 107 us -> 104 us (0.972)
  the two profiles are of different devices: /device:TPU:161 before, /device:TPU:97 now
where the time goes in v3:
time: 104 us
  Pallas kernels  104 us (100%)
    pallas_call x1, Pallas kernels, shards(): pl.pallas_call(functools.partial(kernel, nz), out_shape=results, in_specs...  101 us
    pallas_call x1, Pallas kernels, shards(): pl.pallas_call(hand_over, out_shape=results, in_specs=hbm * 4, out_specs=...  2.77 us

profile of v3, /device:TPU:97, one launch (start us, length us, event | category | flops | bytes accessed | tf_op | source)
XLA Modules:
  0.0 104.3 jit_solution(12535759698478442336)
XLA Ops:
  0.6 100.9 %shard_map.84 = (bf16[512,1024]{1,0:T(8,128)(2,1)}, bf16[512,1024]{1,0:T(8,128)(2,1)}, bf16[8,16,1024]{2,1,0:T(8,128)(2,1)}, bf16[8,16,1024]{2,1,0:T(8,128)(2,1)}) custom-call(s32[71,512]{1,0:T(8,128)} %bitcast.1, bf16[512,1024]{1,0:T(8,128)(2,1)} %q_hbm.1, bf16[8,16,1024]{2,1,0:T(8,128)(2,1)} %k_hbm.1, bf16[8,16,1024]{2,1,0:T(8,128)(2,1)} %v_hbm.1, ...), custom_call_target="tpu_custom_call" | custom-call | tf_op jit(solution)/shard_map/pallas_call | solution.py:745
  101.6 2.8 %shard_map.85 = (bf16[512,1024]{1,0:T(8,128)(2,1)}, bf16[512,1024]{1,0:T(8,128)(2,1)}, bf16[8,16,1024]{2,1,0:T(8,128)(2,1)}, bf16[8,16,1024]{2,1,0:T(8,128)(2,1)}) custom-call(bf16[512,1024]{1,0:T(8,128)(2,1)} %get-tuple-element.8.refs_0_, bf16[512,1024]{1,0:T(8,128)(2,1)} %get-tuple-element.9.refs_1_, bf16[8,16,1024]{2,1,0:T(8,128)(2,1)} %get-tuple-element.10.refs_2_, ...), custom_call_target="tpu_custom_call" | custom-call | tf_op jit(solution)/shard_map/pallas_call | solution.py:818

commit v4 on v3

--- a/solution.py
+++ b/solution.py
@@ -496,8 +496,9 @@
     def far_grad(g):
         h = jnp.where(g >= z, 1, 0)
         j = g - h * z
-        next_at = jnp.minimum(z - 1, 4)
+        next_at = jnp.minimum(z - 1, 5)
         furthest = j - 1 - jnp.where(j > next_at, 1, 0)
+        furthest = jnp.where(is_top, jnp.where(furthest == z - 3, 0, furthest + 1), furthest)
         return jnp.where(j == next_at, z - 1, jnp.where(j == 0, z - 2, furthest)), h
 
     def in_plane(g):
@@ -538,15 +539,18 @@
         @pl.when((g >= 2 * z) & (g < 2 * z + 4))
         def _():
             n = g - 2 * z
-            head, local = n // 2, n % 2 == 1
+            head, local = n // 2, (n == 1) | (n == 2)
             backward(
                 jnp.where(local, nz, z), head, jnp.where(local, 1, 0), jnp.where(local, 0, r * blk - 1), True
             )
 
-            @pl.when(local)
+            @pl.when(n % 2 == 1)
             def _():
                 dq[head] = jnp.transpose(dqt[head] * SCALE).astype(BF16)
                 out_start(*dq_args, head)
+
+            @pl.when(local)
+            def _():
                 fin[head] = grad[nz, head].astype(BF16)
                 for t in range(2):
                     own_fin(head, t).start()

time: 104 us -> 102 us (0.981)
  Pallas kernels: 104 us -> 101 us
    pallas_call x1, Pallas kernels: 101 us -> 98.3 us  [shards(): pl.pallas_call(functools.partial(kernel, nz), out_shape=results, in_specs...]
where the time goes in v4:
time: 102 us
  Pallas kernels  101 us (99%)
    pallas_call x1, Pallas kernels, shards(): pl.pallas_call(functools.partial(kernel, nz), out_shape=results, in_specs...  98.3 us
    pallas_call x1, Pallas kernels, shards(): pl.pallas_call(hand_over, out_shape=results, in_specs=hbm * 4, out_specs=...  2.77 us

profile of v4, /device:TPU:97, one launch (start us, length us, event | category | flops | bytes accessed | tf_op | source)
XLA Modules:
  0.0 101.7 jit_solution(3618082477333411924)
XLA Ops:
  0.6 98.3 %shard_map.84 = (bf16[512,1024]{1,0:T(8,128)(2,1)}, bf16[512,1024]{1,0:T(8,128)(2,1)}, bf16[8,16,1024]{2,1,0:T(8,128)(2,1)}, bf16[8,16,1024]{2,1,0:T(8,128)(2,1)}) custom-call(s32[71,512]{1,0:T(8,128)} %bitcast.1, bf16[512,1024]{1,0:T(8,128)(2,1)} %q_hbm.1, bf16[8,16,1024]{2,1,0:T(8,128)(2,1)} %k_hbm.1, bf16[8,16,1024]{2,1,0:T(8,128)(2,1)} %v_hbm.1, ...), custom_call_target="tpu_custom_call" | custom-call | tf_op jit(solution)/shard_map/pallas_call | solution.py:749
  98.9 2.8 %shard_map.85 = (bf16[512,1024]{1,0:T(8,128)(2,1)}, bf16[512,1024]{1,0:T(8,128)(2,1)}, bf16[8,16,1024]{2,1,0:T(8,128)(2,1)}, bf16[8,16,1024]{2,1,0:T(8,128)(2,1)}) custom-call(bf16[512,1024]{1,0:T(8,128)(2,1)} %get-tuple-element.8.refs_0_, bf16[512,1024]{1,0:T(8,128)(2,1)} %get-tuple-element.9.refs_1_, bf16[8,16,1024]{2,1,0:T(8,128)(2,1)} %get-tuple-element.10.refs_2_, ...), custom_call_target="tpu_custom_call" | custom-call | tf_op jit(solution)/shard_map/pallas_call | solution.py:822

commit v5 on v4

--- a/solution.py
+++ b/solution.py
@@ -227,8 +227,6 @@
             def _(dz=dz, h=h):
                 z_copy(dz, h).start()
 
-    for p in peers:
-        start(kv_copies(p, k))
     m[...] = jnp.full_like(m, -1e30)
     l[...] = jnp.zeros_like(l)
     acc[...] = jnp.zeros_like(acc)
@@ -246,6 +244,9 @@
             @pl.when(is_bottom)
             def _(h=h):
                 wrap_copy(z, h).start()
+
+    for p in peers:
+        start(kv_copies(p, k))
 
     plane_keys = PLANE * blk
 
@@ -327,9 +328,9 @@
 
         @pl.when(it < 4)
         def _():
-            local = it % 2 == 1
-
-            @pl.when(it == 1)
+            local = it >= 2
+
+            @pl.when(it == 2)
             def _():
                 for c in own_kv:
                     c.wait()
@@ -338,7 +339,7 @@
 
             forward(
                 jnp.where(local, nz, z),
-                it // 2,
+                it % 2,
                 jnp.where(local, 1, 0),
                 jnp.where(local, 0, r * blk - 1),
                 True,

time: 102 us -> 102 us (level)
  no operation moved by 1% of the time
where the time goes in v5:
time: 102 us; the launch traced here: 101 us
  Pallas kernels  101 us (99%)
    pallas_call x1, Pallas kernels, shards(): pl.pallas_call(functools.partial(kernel, nz), out_shape=results, in_specs...  97.9 us
    pallas_call x1, Pallas kernels, shards(): pl.pallas_call(hand_over, out_shape=results, in_specs=hbm * 4, out_specs=...  2.77 us

profile of v5, /device:TPU:97, one launch (start us, length us, event | category | flops | bytes accessed | tf_op | source)
XLA Modules:
  0.0 101.4 jit_solution(16490119673611011255)
XLA Ops:
  0.6 97.9 %shard_map.84 = (bf16[512,1024]{1,0:T(8,128)(2,1)}, bf16[512,1024]{1,0:T(8,128)(2,1)}, bf16[8,16,1024]{2,1,0:T(8,128)(2,1)}, bf16[8,16,1024]{2,1,0:T(8,128)(2,1)}) custom-call(s32[71,512]{1,0:T(8,128)} %bitcast.1, bf16[512,1024]{1,0:T(8,128)(2,1)} %q_hbm.1, bf16[8,16,1024]{2,1,0:T(8,128)(2,1)} %k_hbm.1, bf16[8,16,1024]{2,1,0:T(8,128)(2,1)} %v_hbm.1, ...), custom_call_target="tpu_custom_call" | custom-call | tf_op jit(solution)/shard_map/pallas_call | solution.py:750
  98.6 2.8 %shard_map.85 = (bf16[512,1024]{1,0:T(8,128)(2,1)}, bf16[512,1024]{1,0:T(8,128)(2,1)}, bf16[8,16,1024]{2,1,0:T(8,128)(2,1)}, bf16[8,16,1024]{2,1,0:T(8,128)(2,1)}) custom-call(bf16[512,1024]{1,0:T(8,128)(2,1)} %get-tuple-element.8.refs_0_, bf16[512,1024]{1,0:T(8,128)(2,1)} %get-tuple-element.9.refs_1_, bf16[8,16,1024]{2,1,0:T(8,128)(2,1)} %get-tuple-element.10.refs_2_, ...), custom_call_target="tpu_custom_call" | custom-call | tf_op jit(solution)/shard_map/pallas_call | solution.py:823
